TPU v7x, 512 devices: a whole 4x8x8 slice. The times are simulated.
512 devices in a mesh: frame: 16 (over z, core), row: 32 (over y, x).
Axes of the slice: x: 4, y: 8, z: 8, core: 2. Of those that a mesh axis runs over, the one named last changes fastest.
Arguments:
- features: bfloat16 [32, 128, 24, 256], P('frame', 'row'), may hold values from -12 to 12
- norm_gain: float32 [256], replicated, may hold values from 0.5 to 2
- conv_up: bfloat16 [3, 3, 3, 256, 256], replicated, may hold values from -0.078125 to 0.078125
Outputs:
- decoded: bfloat16 [64, 256, 48, 256], P('frame', 'row')
All inputs are finite; a program needn't handle non-finite values.
Results may differ from a plain program's by a relative error of at most 0.0049.
Values may be sent and summed in bfloat16 or wider, within the bound.
A program may use at most 64 MiB of HBM per device.

v0:
```python
import jax
import jax.numpy as jnp
from jax import lax
from jax.sharding import PartitionSpec as P

GROUPS = 32


def shifted(block, axis, distance):
    devices = range(lax.axis_size(axis))
    route = [(i - distance, i) for i in devices if i - distance in devices]
    return lax.ppermute(block, axis, route)


def extended_2(value, sides, width):
    for axis, dim in sides:
        devices, length = (lax.axis_size(axis), value.shape[dim])
        up = [(i, (i + 1) % devices) for i in range(devices - 1)]
        down = [(j, i) for i, j in up]
        last = lax.slice_in_dim(value, length - width, length, axis=dim)
        initial = lax.slice_in_dim(value, 0, width, axis=dim)
        before = lax.ppermute(last, axis, up)
        after = lax.ppermute(initial, axis, down)
        value = jnp.concatenate([before, value, after], axis=dim)
    return value


def conv_taps(padded, weight):
    frame_count = padded.shape[0] - 2
    row_count = padded.shape[1] - 2
    col_count = padded.shape[2] - 2
    running = jnp.zeros((frame_count * row_count * col_count, weight.shape[4]), jnp.float32)
    for tap_t in range(3):
        for tap_h in range(3):
            for tap_w in range(3):
                window = padded[
                    tap_t : tap_t + frame_count,
                    tap_h : tap_h + row_count,
                    tap_w : tap_w + col_count,
                ]
                running = running + jnp.dot(
                    window.reshape(-1, weight.shape[3]),
                    weight[tap_t, tap_h, tap_w],
                    preferred_element_type=jnp.float32,
                )
    return running.reshape(frame_count, row_count, col_count, -1)


def column_pad(volume):
    return jnp.concatenate([volume[:, :, :1], volume, volume[:, :, -1:]], 2)


def time_pad(volume, depth):
    tail_frames = volume[-depth:]
    prior_frames = shifted(tail_frames, "frame", 1)
    is_first = lax.axis_index("frame") == 0
    own_first = jnp.broadcast_to(volume[:1], tail_frames.shape)
    prior_frames = jnp.where(is_first, own_first, prior_frames)
    return jnp.concatenate([prior_frames, volume], 0)


def row_pad(volume):
    extended = extended_2(volume, (("row", 1),), 1)
    row_index = lax.axis_index("row")
    upper_rim = jnp.where(row_index == 0, volume[:, :1], extended[:, :1])
    bottom = jnp.where(row_index == lax.axis_size("row") - 1, volume[:, -1:], extended[:, -1:])
    return jnp.concatenate([upper_rim, volume, bottom], 1)


def causal_pad(volume, depth):
    return column_pad(row_pad(time_pad(volume, depth)))


def upsample(volume):
    return jnp.repeat(jnp.repeat(jnp.repeat(volume, 2, 0), 2, 1), 2, 2)


def shards(features, norm_gain, conv_up):
    frame_count, row_count, col_count, chan_count = features.shape
    group_size = chan_count // GROUPS
    values = features.astype(jnp.float32).reshape(-1, GROUPS, group_size)
    voxel_count = float(
        frame_count
        * lax.axis_size("frame")
        * row_count
        * lax.axis_size("row")
        * col_count
        * group_size
    )
    group_mean = lax.psum(jnp.sum(values, axis=(0, 2)), ("frame", "row")) / voxel_count
    deviation = jnp.sum(jnp.square(values - group_mean[None, :, None]), axis=(0, 2))
    group_var = lax.psum(deviation, ("frame", "row")) / voxel_count
    mean_chan = jnp.repeat(group_mean, group_size)
    inv_chan = jnp.repeat(lax.rsqrt(group_var + 1e-06), group_size)
    activated = jax.nn.silu(
        (features.astype(jnp.float32) - mean_chan) * inv_chan * norm_gain
    ).astype(jnp.bfloat16)
    padded_fine = causal_pad(upsample(activated), 2)
    return conv_taps(padded_fine, conv_up).astype(jnp.bfloat16)


def solution(mesh):
    placed = (P("frame", "row", None, None), P(), P())
    return jax.shard_map(
        shards, mesh=mesh, in_specs=placed, out_specs=P("frame", "row", None, None), check_vma=False
    )
```

profile of v0, /device:TPU:1, one launch (start us, length us, event | category | flops | bytes accessed | tf_op | source)
XLA Modules:
  0.0 240.7 jit_solution(6213877910634510153)
XLA Ops:
  0.0 0.9 convert_reduce_fusion
  1.1 106.1 %psum.14 = f32[32]{0:T(128)S(1)} all-reduce(f32[32]{0:T(128)S(1)} %reduce_sum.25), channel_id=1, replica_groups=mesh['frame'=16,'row'=32] {'frame','row'}, use_global_device_ids=true, to_apply=%region_2.0 | all-reduce | flops 32 | bytes 256 | tf_op jit(solution)/shard_map/psum | solution.py:90
  107.4 0.9 fusion.20
  108.5 0.1 reduce_sum.37
  108.6 93.6 %psum.15 = f32[32]{0:T(128)S(1)} all-reduce(f32[32]{0:T(128)S(1)} %reduce_sum.37), channel_id=1, replica_groups=mesh['frame'=16,'row'=32] {'frame','row'}, use_global_device_ids=true, to_apply=%region_5.6 | all-reduce | flops 32 | bytes 256 | tf_op jit(solution)/shard_map/psum | solution.py:92
  202.4 1.0 fusion.27
  203.6 3.3 %collective-permute-start = (bf16[2,8,48,256]{3,2,1,0:T(8,128)(2,1)S(1)}, bf16[2,8,48,256]{3,2,1,0:T(8,128)(2,1)S(1)}, u32[]{:S(2)}, u32[]{:S(2)}) collective-permute-start(bf16[2,8,48,256]{3,2,1,0:T(8,128)(2,1)S(1)} %broadcast_in_dim.52), channel_id=1, source_target_pairs={{0,32},{32,64},{64,96},{96,128},{128,160},{160,192},{192,224},{224... | collective-permute-start | bytes 1179656 | tf_op jit(solution)/shard_map/ppermute | solution.py:12
  207.2 0.5 broadcast_in_dim.54
  207.6 0.3 reshape.113
  207.9 3.6 %collective-permute-done = bf16[2,8,48,256]{3,2,1,0:T(8,128)(2,1)S(1)} collective-permute-done((bf16[2,8,48,256]{3,2,1,0:T(8,128)(2,1)S(1)}, bf16[2,8,48,256]{3,2,1,0:T(8,128)(2,1)S(1)}, u32[]{:S(2)}, u32[]{:S(2)}) %collective-permute-start) | collective-permute-done | bytes 393248 | tf_op jit(solution)/shard_map/ppermute | solution.py:12
  211.6 3.7 %collective-permute-start.1 = (bf16[6,1,48,256]{3,2,1,0:T(8,128)(2,1)S(1)}, bf16[6,1,48,256]{3,2,1,0:T(8,128)(2,1)S(1)}, u32[]{:S(2)}, u32[]{:S(2)}) collective-permute-start(bf16[6,1,48,256]{3,2,1,0:T(8,128)(2,1)S(1)} %pad_maximum_fusion.8), channel_id=1, source_target_pairs={{0,1},{1,2},{2,3},{3,4},{4,5},{5,6},{6,7},{7,8},{8,9},{9,10},{10,1... | collective-permute-start | bytes 442376 | tf_op jit(solution)/shard_map/ppermute | solution.py:22
  215.3 0.3 reshape_reshape.3
  215.6 1.8 collective-permute-done.1
  217.4 1.5 collective-permute-start.2
  219.0 4.7 %collective-permute-done.2 = bf16[6,1,48,256]{3,2,1,0:T(8,128)(2,1)S(1)} collective-permute-done((bf16[6,1,48,256]{3,2,1,0:T(8,128)(2,1)S(1)}, bf16[6,1,48,256]{3,2,1,0:T(8,128)(2,1)S(1)}, u32[]{:S(2)}, u32[]{:S(2)}) %collective-permute-start.2) | collective-permute-done | bytes 147488 | tf_op jit(solution)/shard_map/ppermute | solution.py:23
  223.8 0.2 pad_maximum_fusion.6
  224.0 1.9 fusion.10
  225.9 0.7 fusion.84
  226.5 1.1 fusion.83
  227.7 0.5 fusion.85
  228.2 1.5 copy-done
  229.7 0.4 fusion.54
  230.0 0.4 convolution_add_fusion.25
  230.4 0.4 convolution_add_fusion.24
  230.8 0.4 convolution_add_fusion.23
  231.1 0.4 convolution_add_fusion.22
  231.5 0.4 convolution_add_fusion.21
  231.9 0.4 convolution_add_fusion.20
  232.3 0.4 convolution_add_fusion.19
  232.7 0.4 convolution_add_fusion.18
  233.0 0.4 convolution_add_fusion.17
  233.4 0.4 convolution_add_fusion.16
  233.8 0.4 convolution_add_fusion.15
  234.2 0.4 convolution_add_fusion.14
  234.6 0.4 convolution_add_fusion.13
  234.9 0.4 convolution_add_fusion.12
  235.3 0.4 convolution_add_fusion.11
  235.7 0.4 convolution_add_fusion.10
  236.1 0.4 convolution_add_fusion.9
  236.4 0.4 convolution_add_fusion.8
  236.8 0.4 convolution_add_fusion.7
  237.2 0.4 convolution_add_fusion.6
  237.6 0.4 convolution_add_fusion.5
  238.0 0.4 convolution_add_fusion.4
  238.3 0.4 convolution_add_fusion.3
  238.7 0.4 convolution_add_fusion.2
  239.1 0.4 convolution_add_fusion.1
  239.5 1.3 fusion.8
  (26 shorter events, 1.3 us)
Async XLA Ops:
  203.6 8.0 %collective-permute-start = (bf16[2,8,48,256]{3,2,1,0:T(8,128)(2,1)S(1)}, bf16[2,8,48,256]{3,2,1,0:T(8,128)(2,1)S(1)}, u32[]{:S(2)}, u32[]{:S(2)}) collective-permute-start(bf16[2,8,48,256]{3,2,1,0:T(8,128)(2,1)S(1)} %broadcast_in_dim.52), channel_id=1, source_target_pairs={{0,32},{32,64},{64,96},{96,128},{128,160},{160,192},{192,224},{224... | collective-permute-start | bytes 1179656 | tf_op jit(solution)/shard_map/ppermute | solution.py:12
  211.6 5.8 %collective-permute-start.1 = (bf16[6,1,48,256]{3,2,1,0:T(8,128)(2,1)S(1)}, bf16[6,1,48,256]{3,2,1,0:T(8,128)(2,1)S(1)}, u32[]{:S(2)}, u32[]{:S(2)}) collective-permute-start(bf16[6,1,48,256]{3,2,1,0:T(8,128)(2,1)S(1)} %pad_maximum_fusion.8), channel_id=1, source_target_pairs={{0,1},{1,2},{2,3},{3,4},{4,5},{5,6},{6,7},{7,8},{8,9},{9,10},{10,1... | collective-permute-start | bytes 442376 | tf_op jit(solution)/shard_map/ppermute | solution.py:22
  217.4 6.3 %collective-permute-start.2 = (bf16[6,1,48,256]{3,2,1,0:T(8,128)(2,1)S(1)}, bf16[6,1,48,256]{3,2,1,0:T(8,128)(2,1)S(1)}, u32[]{:S(2)}, u32[]{:S(2)}) collective-permute-start(bf16[6,1,48,256]{3,2,1,0:T(8,128)(2,1)S(1)} %get-tuple-element.6), channel_id=1, source_target_pairs={{1,0},{2,1},{3,2},{4,3},{5,4},{6,5},{7,6},{8,7},{9,8},{10,9},{11,1... | collective-permute-start | bytes 442376 | tf_op jit(solution)/shard_map/ppermute | solution.py:23
  227.6 2.0 copy-start
where the time goes:
time: 244 us; the launch traced here: 241 us
  blocking collectives  200 us (82%)
  matrix products  10.9 us (4%)
  waiting for transfers between devices  10.1 us (4%)
  starting transfers between devices  8.43 us (3%)
  local copies, waits for them, and re-layouts  5.76 us (2%)
  other arithmetic  5.36 us (2%)
    psum x1, blocking collectives, shards(): lax.psum(jnp.sum(values, axis=(0, 2)), ('frame', 'row')) / voxel_count  106 us
    psum x1, blocking collectives, shards(): group_var = lax.psum(deviation, ('frame', 'row')) / voxel_count  93.6 us
    dot_general x27, matrix products, conv_taps(): jnp.dot(window.reshape(-1, weight.shape[3]), weight[tap_t, tap_h, tap_w],...  10.9 us
  transfers between devices with their start and end apart: 3, of which 3 were waited for; matrix products, arithmetic and copies ran while one was open for 1% of the time, Pallas kernels for 0%

commit v1 on v0

v1 whole, which is shorter than its diff:
```python
import functools

import jax
import jax.numpy as jnp
from jax import lax
from jax.experimental import pallas as pl
from jax.experimental.pallas import tpu as pltpu
from jax.sharding import PartitionSpec as P

MESH = pl.DeviceIdType.MESH
GROUP = 8
F32, BF16 = jnp.float32, jnp.bfloat16


def lane_index(shape):
    return lax.broadcasted_iota(jnp.int32, shape, len(shape) - 1)


def swapped(value, distance):
    upper = (lane_index(value.shape) & distance) == 0
    return jnp.where(upper, pltpu.roll(value, 128 - distance, 1), pltpu.roll(value, distance, 1))


def local_statistics(own, rows):
    count = float(rows)
    mean = jnp.sum(own, axis=0, keepdims=True) * (1.0 / count)
    spread = jnp.sum(jnp.square(own - mean), axis=0, keepdims=True)
    packed = jnp.zeros((8, 128), F32)
    kind = lane_index((8, 128)) & 7
    for half in range(2):
        lanes = slice(128 * half, 128 * half + 128)
        m = jnp.broadcast_to(mean[:, lanes], (8, 128))
        s = jnp.broadcast_to(spread[:, lanes], (8, 128))
        held = count
        for distance in (1, 2, 4):
            other_m, other_s = swapped(m, distance), swapped(s, distance)
            s = s + other_s + (0.5 * held) * jnp.square(m - other_m)
            m = 0.5 * (m + other_m)
            held *= 2.0
        packed = jnp.where(kind == half, m, jnp.where(kind == 2 + half, s, packed))
    return packed[0:1]


def merged(parts, count):
    total = jnp.sum(parts, axis=0)
    mean = total * (1.0 / parts.shape[0])
    apart = jnp.sum(jnp.square(parts - mean[None]), axis=0)
    apart = pltpu.roll(jnp.broadcast_to(apart, (8, 128)), 2, 1)[0:1]
    kind = lane_index((1, 128)) & 7
    return jnp.where(kind < 2, mean, total + count * apart)


def comm_kernel(
    shape, feat, weight, gain, halo_out, stat_out, folded,
    raw, held, scale, msg1, buf1, msg2, buf2, in_sem, send1, recv1, send2, recv2, halo_send, halo_recv,
):
    frames, ydim, xdim, total = shape
    rows = ydim * xdim
    f, r = lax.axis_index("frame"), lax.axis_index("row")
    y, x = r // xdim, r % xdim
    own = held.at[1:3, 48:144]

    load = pltpu.make_async_copy(feat, own, in_sem.at[0])
    load.start()

    def plane(i):
        return ((y + i // xdim) % ydim) * xdim + (x + i) % xdim

    barrier = pltpu.get_barrier_semaphore()

    def greet_plane(i, carry):
        pl.semaphore_signal(barrier, inc=1, device_id=(f, plane(i)), device_id_type=MESH)
        return carry

    def greet_later(k, carry):
        pl.semaphore_signal(barrier, inc=1, device_id=(k, r), device_id_type=MESH)
        return carry

    lax.fori_loop(f + 1, frames, greet_later, 0)
    lax.fori_loop(1, rows, greet_plane, 0)

    fetch = pltpu.make_async_copy(weight, raw, in_sem.at[1])
    fetch.start()
    gains = pltpu.make_async_copy(gain, scale, in_sem.at[2])
    gains.start()

    load.wait()
    values = held[1:3, 48:144].astype(F32).reshape(192, 256)
    mine = local_statistics(values, 192)
    msg1[...] = mine
    buf1[f] = mine
    pl.semaphore_wait(barrier, rows - 1 + f)

    def send_first(k, carry):
        pltpu.make_async_remote_copy(
            src_ref=msg1, dst_ref=buf1.at[f], send_sem=send1, recv_sem=recv1.at[f],
            device_id=(k, r), device_id_type=MESH,
        ).start()
        return carry

    lax.fori_loop(0, f, send_first, 0)

    down = pltpu.make_async_remote_copy(
        src_ref=held.at[1:3, 96:144], dst_ref=held.at[1:3, 0:48], send_sem=halo_send.at[0],
        recv_sem=halo_recv.at[0], device_id=(f, (r + 1) % rows), device_id_type=MESH,
    )
    up = pltpu.make_async_remote_copy(
        src_ref=held.at[1:3, 48:96], dst_ref=held.at[1:3, 144:192], send_sem=halo_send.at[1],
        recv_sem=halo_recv.at[1], device_id=(f, (r + rows - 1) % rows), device_id_type=MESH,
    )
    down.start()
    up.start()

    fetch.wait()
    gains.wait()

    def fold(step, carry):
        at = pl.multiple_of(step * 16, 16)
        for half in range(2):
            lanes = slice(128 * half, 128 * half + 128)
            for kind in range(3):
                def tap(h, w):
                    if kind == 0:
                        return raw[h * 3 + w, pl.ds(at, 16), lanes].astype(F32) + raw[
                            9 + h * 3 + w, pl.ds(at, 16), lanes].astype(F32)
                    return raw[(18 if kind == 1 else 9) + h * 3 + w, pl.ds(at, 16), lanes].astype(F32)

                t = [[tap(h, w) for w in range(3)] for h in range(3)]
                by_row = [[t[0], [t[1][w] + t[2][w] for w in range(3)]],
                          [[t[0][w] + t[1][w] for w in range(3)], t[2]]]
                for p in range(2):
                    for a in range(2):
                        u = by_row[p][a]
                        by_col = [[u[0], u[1] + u[2]], [u[0] + u[1], u[2]]]
                        for q in range(2):
                            for b in range(2):
                                base = kind * 1024 + (a * 2 + b) * 256
                                folded[p * 2 + q, pl.ds(base + at, 16), lanes] = by_col[q][b].astype(BF16)
        return carry

    lax.fori_loop(0, 16, fold, 0)

    def answer(k, carry):
        pltpu.make_async_copy(buf1.at[k], buf1.at[k], recv1.at[k]).wait()
        pltpu.make_async_remote_copy(
            src_ref=msg1, dst_ref=buf1.at[f], send_sem=send1, recv_sem=recv1.at[f],
            device_id=(k, r), device_id_type=MESH,
        ).start()
        return carry

    lax.fori_loop(f + 1, frames, answer, 0)
    down.wait_recv()
    up.wait_recv()
    forward = pltpu.make_async_remote_copy(
        src_ref=held.at[2], dst_ref=held.at[0], send_sem=halo_send.at[2], recv_sem=halo_recv.at[2],
        device_id=((f + 1) % frames, r), device_id_type=MESH,
    )

    @pl.when(f + 1 < frames)
    def _():
        forward.start()

    def collect(k, carry):
        pltpu.make_async_copy(buf1.at[k], buf1.at[k], recv1.at[k]).wait()
        return carry

    lax.fori_loop(0, f, collect, 0)
    line = merged(buf1[...], 192.0 * GROUP)
    msg2[...] = line
    buf2[r] = line

    def send_second(i, carry):
        pltpu.make_async_remote_copy(
            src_ref=msg2, dst_ref=buf2.at[r], send_sem=send2, recv_sem=recv2,
            device_id=(f, plane(i)), device_id_type=MESH,
        ).start()
        return carry

    lax.fori_loop(rows // 2, rows, send_second, 0)
    lax.fori_loop(1, rows // 2, send_second, 0)

    @pl.when(f > 0)
    def _():
        forward.wait_recv()

    @pl.when(f == 0)
    def _():
        held[0] = held[1]

    halo_out[...] = held[...]
    others = buf2.at[0:rows - 1]
    pltpu.make_async_copy(others, others, recv2).wait()
    line = jnp.broadcast_to(merged(buf2[...], 192.0 * GROUP * frames), (8, 128))
    kind = lane_index((8, 128)) & 7
    spread = []
    for k in range(4):
        v = jnp.where(kind == k, line, 0.0)
        for distance in (1, 2, 4):
            v = v + swapped(v, distance)
        spread.append(v[0:1])
    var = jnp.concatenate(spread[2:], axis=1) * (1.0 / total)
    stat_out[0:1] = jnp.concatenate(spread[:2], axis=1)
    stat_out[1:2] = lax.rsqrt(var + 1e-06) * scale[...]

    sent = buf1.at[0:frames - 1]
    pltpu.make_async_copy(sent, sent, send1).wait()
    pltpu.make_async_copy(others, others, send2).wait()
    down.wait_send()
    up.wait_send()

    @pl.when(f + 1 < frames)
    def _():
        forward.wait_send()


def conv_kernel(shape, halo, stat, folded, out, act, even_rows, odd_rows, wide, staged, out_sem):
    rows = shape
    r = lax.axis_index("row")

    mean, scale = stat[0:1], stat[1:2]
    for t in range(3):
        v = (halo[t, :, :].astype(F32)[24:168] - mean) * scale
        v = (v / (1.0 + jnp.exp(-v))).astype(BF16).astype(F32).reshape(6, 24, 256)
        top = jnp.where(r == 0, v[1:2], v[0:1])
        bottom = jnp.where(r == rows - 1, v[4:5], v[5:6])
        v = jnp.concatenate([top, v[1:5], bottom], axis=0)
        act[t, :, 8:32, :] = v
        act[t, :, 7:8, :] = v[:, 0:1]
        act[t, :, 32:33, :] = v[:, 23:24]
    for s in range(3):
        v = [act[t, :, 7 + s:31 + s, :] for t in range(3)]
        v = v + [v[1] - v[0], v[2] - v[1]]
        for t in range(5):
            even_rows[s, t] = v[t].reshape(144, 256).astype(BF16)
            odd_rows[s, t] = v[t][1:5].reshape(96, 256).astype(BF16)

    def piece(kind, sr, sc):
        first = (0, 1, 3)[kind]
        if sr == 1:
            return odd_rows[sc, first:first + 2].reshape(192, 256)
        return even_rows[sc, first:first + 2, 24 * sr:24 * sr + 96].reshape(192, 256)

    copies = []
    for p in range(2):
        for q in range(2):
            def taps(kind):
                return [piece(kind, p + a, q + b) for a in range(2) for b in range(2)]

            first = jnp.dot(jnp.concatenate(taps(0) + taps(1), axis=1), folded[p * 2 + q, 0:2048],
                            preferred_element_type=F32)
            step = jnp.dot(jnp.concatenate(taps(2), axis=1), folded[p * 2 + q, 2048:3072],
                           preferred_element_type=F32)
            second = first + step
            for i in range(2):
                for alpha, v in enumerate((first, second)):
                    for half in range(2):
                        lanes = slice(128 * half, 128 * half + 128)
                        wide[half, 2 * i + alpha, :, pl.ds(q, 24, 2), :] = v[96 * i:96 * i + 96, lanes].reshape(
                            4, 24, 128)
        for half in range(2):
            staged[p, :, :, :, 128 * half:128 * half + 128] = wide[half].astype(BF16)
        copy = pltpu.make_async_copy(staged.at[p], out.at[:, :, p], out_sem.at[p])
        copy.start()
        copies.append(copy)
    for copy in copies:
        copy.wait()


def solution(mesh):
    frames, rows = mesh.shape["frame"], mesh.shape["row"]
    xdim = 4 if rows % 4 == 0 else 1
    any_, vmem = pl.BlockSpec(memory_space=pltpu.HBM), pl.BlockSpec(memory_space=pltpu.VMEM)

    def shards(features, norm_gain, conv_up):
        voxels = float(192 * GROUP * frames * rows)
        halo, stat, folded = pl.pallas_call(
            functools.partial(comm_kernel, (frames, rows // xdim, xdim, voxels)),
            out_shape=(pltpu.VMEM((3, 192, 256), BF16), pltpu.VMEM((2, 256), F32), pltpu.VMEM((4, 3072, 256), BF16)),
            in_specs=[any_, any_, any_],
            out_specs=(vmem, vmem, vmem),
            scratch_shapes=[
                pltpu.VMEM((27, 256, 256), BF16),
                pltpu.VMEM((3, 192, 256), BF16),
                pltpu.VMEM((1, 256), F32),
                pltpu.VMEM((1, 128), F32),
                pltpu.VMEM((frames, 1, 128), F32),
                pltpu.VMEM((1, 128), F32),
                pltpu.VMEM((rows, 1, 128), F32),
                pltpu.SemaphoreType.DMA((3,)),
                pltpu.SemaphoreType.DMA,
                pltpu.SemaphoreType.DMA((frames,)),
                pltpu.SemaphoreType.DMA,
                pltpu.SemaphoreType.DMA,
                pltpu.SemaphoreType.DMA((3,)),
                pltpu.SemaphoreType.DMA((3,)),
            ],
            compiler_params=pltpu.CompilerParams(
                collective_id=0, has_side_effects=True, vmem_limit_bytes=54 * 2**20),
            name="statistics",
        )(features.reshape(2, 96, 256), conv_up.reshape(27, 256, 256), norm_gain.reshape(1, 256))
        out = pl.pallas_call(
            functools.partial(conv_kernel, rows),
            out_shape=jax.ShapeDtypeStruct((4, 4, 2, 48, 256), BF16),
            in_specs=[vmem, vmem, vmem],
            out_specs=any_,
            scratch_shapes=[
                pltpu.VMEM((3, 6, 40, 256), F32),
                pltpu.VMEM((3, 5, 144, 256), BF16),
                pltpu.VMEM((3, 5, 96, 256), BF16),
                pltpu.VMEM((2, 4, 4, 48, 128), F32),
                pltpu.VMEM((2, 4, 4, 48, 256), BF16),
                pltpu.SemaphoreType.DMA((2,)),
            ],
            compiler_params=pltpu.CompilerParams(vmem_limit_bytes=24 * 2**20),
            name="conv",
        )(halo, stat, folded)
        return out.reshape(4, 8, 48, 256)

    spec = P("frame", "row", None, None)
    return jax.shard_map(shards, mesh=mesh, in_specs=(spec, P(), P()), out_specs=spec, check_vma=False)
```

time: 244 us -> 26.6 us (0.11); the launches traced: 241 us -> 26.5 us
  blocking collectives: 200 us -> 0 us
  Pallas kernels: 0 us -> 26.5 us
  matrix products: 10.9 us -> 0 us
  waiting for transfers between devices: 10.1 us -> 0 us
  starting transfers between devices: 8.43 us -> 0 us
  local copies, waits for them, and re-layouts: 5.76 us -> 0 us
  other arithmetic: 5.36 us -> 0 us
    psum x2 -> x0, blocking collectives: 200 us -> none  [the longest x1 106 us: shards(): lax.psum(jnp.sum(values, axis=(0, 2)), ('frame', 'row')) / voxel_count]
    pallas_call x0 -> x2, Pallas kernels: none -> 26.5 us  [the longest x1 24 us: shards(): pl.pallas_call(functools.partial(comm_kernel, (frames, rows // xdim, xdim...]
    dot_general x27 -> x0, matrix products: 10.9 us -> none  [conv_taps(): jnp.dot(window.reshape(-1, weight.shape[3]), weight[tap_t, tap_h, tap_w],...]
    ppermute x3 -> x0, waiting for transfers between devices: 10.1 us -> none  [the longest x1 4.73 us: extended_2(): after = lax.ppermute(initial, axis, down)]
    ppermute x3 -> x0, starting transfers between devices: 8.43 us -> none  [the longest x1 3.69 us: extended_2(): before = lax.ppermute(last, axis, up)]
  transfers between devices with their start and end apart: 3 -> 0, of which waited for: 3 -> 0; matrix products, arithmetic and copies ran while one was open for 1% -> 0% of each run, Pallas kernels for 0% -> 0%
where the time goes in v1:
time: 26.6 us; the launch traced here: 26.5 us
  Pallas kernels  26.5 us (100%)
    pallas_call x1, Pallas kernels, shards(): pl.pallas_call(functools.partial(comm_kernel, (frames, rows // xdim, xdim...  24 us
    pallas_call x1, Pallas kernels, shards(): pl.pallas_call(functools.partial(conv_kernel, rows), out_shape=jax.ShapeD...  2.51 us

profile of v1, /device:TPU:1, one launch (start us, length us, event | category | flops | bytes accessed | tf_op | source)
XLA Modules:
  0.0 26.5 jit_solution(11372212458700712005)
XLA Ops:
  0.0 24.0 %statistics.1 = (bf16[3,192,256]{2,1,0:T(8,128)(2,1)S(1)}, f32[2,256]{1,0:T(2,128)S(1)}, bf16[4,3072,256]{2,1,0:T(8,128)(2,1)S(1)}) custom-call(bf16[2,96,256]{2,1,0:T(8,128)(2,1)} %bitcast.5, bf16[27,256,256]{2,1,0:T(8,128)(2,1)} %bitcast.4, f32[1,256]{1,0:T(1,128)} %bitcast.6), custom_call_target="tpu_custom_call" | custom-call | tf_op jit(solution)/shard_map/statistics/pallas_call | solution.py:276
  24.0 2.5 %conv.1 = bf16[4,4,2,48,256]{4,3,2,1,0:T(8,128)(2,1)} custom-call(bf16[3,192,256]{2,1,0:T(8,128)(2,1)S(1)} %get-tuple-element.8.halo, f32[2,256]{1,0:T(2,128)S(1)} %get-tuple-element.9.stat, bf16[4,3072,256]{2,1,0:T(8,128)(2,1)S(1)} %get-tuple-element.10.folded), custom_call_target="tpu_custom_call" | custom-call | tf_op jit(solution)/shard_map/conv/pallas_call | solution.py:301

commit v2 on v1

--- a/solution.py
+++ b/solution.py
@@ -10,6 +10,8 @@
 MESH = pl.DeviceIdType.MESH
 GROUP = 8
 F32, BF16 = jnp.float32, jnp.bfloat16
+ROOT = 1
+LATE = 6
 
 
 def lane_index(shape):
@@ -52,64 +54,110 @@
 
 def comm_kernel(
     shape, feat, weight, gain, halo_out, stat_out, folded,
-    raw, held, scale, msg1, buf1, msg2, buf2, in_sem, send1, recv1, send2, recv2, halo_send, halo_recv,
+    raw, held, scale, msg1, buf1, lines, final,
+    in_sem, send1, recv1, send3, recv3, halo_send, halo_recv, ready,
 ):
     frames, ydim, xdim, total = shape
     rows = ydim * xdim
     f, r = lax.axis_index("frame"), lax.axis_index("row")
     y, x = r // xdim, r % xdim
-    own = held.at[1:3, 48:144]
-
-    load = pltpu.make_async_copy(feat, own, in_sem.at[0])
-    load.start()
+    is_root = f == ROOT
+
+    loads = [
+        pltpu.make_async_copy(feat.at[t, part], held.at[1 + t, pl.ds(48 + part.start, 48)], in_sem.at[2 + 2 * t + i])
+        for t in range(2) for i, part in enumerate((slice(0, 48), slice(48, 96)))
+    ]
+    for load in loads:
+        load.start()
+
+    def order(row):
+        return row % xdim * rows + row
+
+    below, above = (r + 1) % rows, (r + rows - 1) % rows
+    below_later, above_later = order(below) > order(r), order(above) > order(r)
 
     def plane(i):
         return ((y + i // xdim) % ydim) * xdim + (x + i) % xdim
 
+    def to_root(i):
+        return pltpu.make_async_remote_copy(
+            src_ref=msg1, dst_ref=buf1.at[f, r], send_sem=send1, recv_sem=recv1.at[f],
+            device_id=(ROOT, plane(i)), device_id_type=MESH,
+        )
+
     barrier = pltpu.get_barrier_semaphore()
 
+    def greet(frame, row):
+        pl.semaphore_signal(barrier, inc=1, device_id=(frame, row), device_id_type=MESH)
+
     def greet_plane(i, carry):
-        pl.semaphore_signal(barrier, inc=1, device_id=(f, plane(i)), device_id_type=MESH)
+        greet(f, plane(i))
         return carry
 
-    def greet_later(k, carry):
-        pl.semaphore_signal(barrier, inc=1, device_id=(k, r), device_id_type=MESH)
+    def greet_line(k, carry):
+        greet(k, r)
         return carry
 
-    lax.fori_loop(f + 1, frames, greet_later, 0)
-    lax.fori_loop(1, rows, greet_plane, 0)
-
-    fetch = pltpu.make_async_copy(weight, raw, in_sem.at[1])
-    fetch.start()
-    gains = pltpu.make_async_copy(gain, scale, in_sem.at[2])
-    gains.start()
-
-    load.wait()
+    @pl.when(is_root)
+    def _():
+        lax.fori_loop(1, rows, greet_plane, 0)
+
+    @pl.when(jnp.logical_not(is_root))
+    def _():
+        @pl.when(below_later)
+        def _():
+            greet(f, below)
+
+        @pl.when(above_later)
+        def _():
+            greet(f, above)
+
+    for load in loads:
+        load.wait()
     values = held[1:3, 48:144].astype(F32).reshape(192, 256)
     mine = local_statistics(values, 192)
     msg1[...] = mine
-    buf1[f] = mine
-    pl.semaphore_wait(barrier, rows - 1 + f)
-
-    def send_first(k, carry):
-        pltpu.make_async_remote_copy(
-            src_ref=msg1, dst_ref=buf1.at[f], send_sem=send1, recv_sem=recv1.at[f],
-            device_id=(k, r), device_id_type=MESH,
-        ).start()
+    pl.semaphore_wait(barrier, jnp.where(
+        is_root, rows - 1, 3 - below_later.astype(jnp.int32) - above_later.astype(jnp.int32)))
+
+    @pl.when(is_root)
+    def _():
+        buf1[ROOT, r] = mine
+        greet(0, r)
+        lax.fori_loop(ROOT + 1, frames, greet_line, 0)
+
+    @pl.when(jnp.logical_not(is_root))
+    def _():
+        to_root(0).start()
+
+    def to_others(i, carry):
+        to_root(i).start()
         return carry
 
-    lax.fori_loop(0, f, send_first, 0)
+    lax.fori_loop(rows // 2, rows, to_others, 0)
+    lax.fori_loop(1, rows // 2, to_others, 0)
+
+    fetch = pltpu.make_async_copy(weight, raw, in_sem.at[0])
+    fetch.start()
+    gains = pltpu.make_async_copy(gain, scale, in_sem.at[1])
+    gains.start()
 
     down = pltpu.make_async_remote_copy(
         src_ref=held.at[1:3, 96:144], dst_ref=held.at[1:3, 0:48], send_sem=halo_send.at[0],
-        recv_sem=halo_recv.at[0], device_id=(f, (r + 1) % rows), device_id_type=MESH,
+        recv_sem=halo_recv.at[0], device_id=(f, below), device_id_type=MESH,
     )
     up = pltpu.make_async_remote_copy(
         src_ref=held.at[1:3, 48:96], dst_ref=held.at[1:3, 144:192], send_sem=halo_send.at[1],
-        recv_sem=halo_recv.at[1], device_id=(f, (r + rows - 1) % rows), device_id_type=MESH,
+        recv_sem=halo_recv.at[1], device_id=(f, above), device_id_type=MESH,
     )
-    down.start()
-    up.start()
+
+    @pl.when(jnp.logical_not(below_later))
+    def _():
+        down.start()
+
+    @pl.when(jnp.logical_not(above_later))
+    def _():
+        up.start()
 
     fetch.wait()
     gains.wait()
@@ -140,57 +188,102 @@
 
     lax.fori_loop(0, 16, fold, 0)
 
-    def answer(k, carry):
-        pltpu.make_async_copy(buf1.at[k], buf1.at[k], recv1.at[k]).wait()
-        pltpu.make_async_remote_copy(
-            src_ref=msg1, dst_ref=buf1.at[f], send_sem=send1, recv_sem=recv1.at[f],
-            device_id=(k, r), device_id_type=MESH,
-        ).start()
-        return carry
-
-    lax.fori_loop(f + 1, frames, answer, 0)
-    down.wait_recv()
-    up.wait_recv()
+    @pl.when(below_later)
+    def _():
+        up.wait_recv()
+        down.start()
+
+    @pl.when(above_later)
+    def _():
+        down.wait_recv()
+        up.start()
+
+    @pl.when(jnp.logical_not(below_later))
+    def _():
+        up.wait_recv()
+
+    @pl.when(jnp.logical_not(above_later))
+    def _():
+        down.wait_recv()
+
     forward = pltpu.make_async_remote_copy(
         src_ref=held.at[2], dst_ref=held.at[0], send_sem=halo_send.at[2], recv_sem=halo_recv.at[2],
         device_id=((f + 1) % frames, r), device_id_type=MESH,
     )
 
-    @pl.when(f + 1 < frames)
-    def _():
-        forward.start()
-
-    def collect(k, carry):
+    def arrived(k):
         pltpu.make_async_copy(buf1.at[k], buf1.at[k], recv1.at[k]).wait()
-        return carry
-
-    lax.fori_loop(0, f, collect, 0)
-    line = merged(buf1[...], 192.0 * GROUP)
-    msg2[...] = line
-    buf2[r] = line
-
-    def send_second(i, carry):
-        pltpu.make_async_remote_copy(
-            src_ref=msg2, dst_ref=buf2.at[r], send_sem=send2, recv_sem=recv2,
-            device_id=(f, plane(i)), device_id_type=MESH,
-        ).start()
-        return carry
-
-    lax.fori_loop(rows // 2, rows, send_second, 0)
-    lax.fori_loop(1, rows // 2, send_second, 0)
-
-    @pl.when(f > 0)
-    def _():
-        forward.wait_recv()
-
-    @pl.when(f == 0)
-    def _():
-        held[0] = held[1]
-
-    halo_out[...] = held[...]
-    others = buf2.at[0:rows - 1]
-    pltpu.make_async_copy(others, others, recv2).wait()
-    line = jnp.broadcast_to(merged(buf2[...], 192.0 * GROUP * frames), (8, 128))
+
+    def pass_on():
+        @pl.when(f + 1 < frames)
+        def _():
+            forward.start()
+
+        @pl.when(f > 0)
+        def _():
+            forward.wait_recv()
+
+        @pl.when(f == 0)
+        def _():
+            held[0] = held[1]
+
+        halo_out[...] = held[...]
+
+    others = buf1.at[ROOT, 0:rows - 1]
+    heard = final.at[0:frames - 1]
+
+    @pl.when(is_root)
+    def _():
+        def gather(k):
+            lines[k] = merged(buf1[k], 192.0 * GROUP)
+
+        def tell(k):
+            pl.semaphore_signal(ready, inc=1, device_id=(k - 1, r), device_id_type=MESH)
+
+        pltpu.make_async_copy(others, others, recv1.at[ROOT]).wait()
+        gather(ROOT)
+        for k in (0, ROOT + 1):
+            arrived(k)
+            gather(k)
+        pass_on()
+
+        def collect(k, carry):
+            arrived(k)
+            tell(k)
+            gather(k)
+            return carry
+
+        def collect_late(k, carry):
+            arrived(k)
+            tell(k)
+            return carry
+
+        lax.fori_loop(ROOT + 2, frames - LATE, collect, 0)
+        lax.fori_loop(frames - LATE, frames, collect_late, 0)
+        for k in range(frames - LATE, frames):
+            gather(k)
+        final[0] = merged(lines[...], 192.0 * GROUP * rows)
+
+        def send_third(k, carry):
+            pltpu.make_async_remote_copy(
+                src_ref=final.at[0], dst_ref=final.at[0], send_sem=send3, recv_sem=recv3,
+                device_id=(k, r), device_id_type=MESH,
+            ).start()
+            return carry
+
+        send_third(0, 0)
+        lax.fori_loop(ROOT + 1, frames, send_third, 0)
+
+    @pl.when(jnp.logical_not(is_root))
+    def _():
+        @pl.when((f > ROOT) & (f + 1 < frames))
+        def _():
+            pl.semaphore_wait(ready, 1)
+
+        pass_on()
+        pltpu.make_async_copy(final.at[0], final.at[0], recv3).wait()
+
+    line = jnp.broadcast_to(final[0], (8, 128))
     kind = lane_index((8, 128)) & 7
     spread = []
     for k in range(4):
@@ -202,9 +295,15 @@
     stat_out[0:1] = jnp.concatenate(spread[:2], axis=1)
     stat_out[1:2] = lax.rsqrt(var + 1e-06) * scale[...]
 
-    sent = buf1.at[0:frames - 1]
-    pltpu.make_async_copy(sent, sent, send1).wait()
-    pltpu.make_async_copy(others, others, send2).wait()
+    @pl.when(jnp.logical_not(is_root))
+    def _():
+        pltpu.make_async_copy(buf1.at[0], buf1.at[0], send1).wait()
+
+    @pl.when(is_root)
+    def _():
+        pltpu.make_async_copy(others, others, send1).wait()
+        pltpu.make_async_copy(heard, heard, send3).wait()
+
     down.wait_send()
     up.wait_send()
 
@@ -283,16 +382,17 @@
                 pltpu.VMEM((3, 192, 256), BF16),
                 pltpu.VMEM((1, 256), F32),
                 pltpu.VMEM((1, 128), F32),
+                pltpu.VMEM((frames, rows, 1, 128), F32),
                 pltpu.VMEM((frames, 1, 128), F32),
-                pltpu.VMEM((1, 128), F32),
-                pltpu.VMEM((rows, 1, 128), F32),
-                pltpu.SemaphoreType.DMA((3,)),
+                pltpu.VMEM((frames - 1, 1, 128), F32),
+                pltpu.SemaphoreType.DMA((6,)),
                 pltpu.SemaphoreType.DMA,
                 pltpu.SemaphoreType.DMA((frames,)),
                 pltpu.SemaphoreType.DMA,
                 pltpu.SemaphoreType.DMA,
                 pltpu.SemaphoreType.DMA((3,)),
                 pltpu.SemaphoreType.DMA((3,)),
+                pltpu.SemaphoreType.REGULAR,
             ],
             compiler_params=pltpu.CompilerParams(
                 collective_id=0, has_side_effects=True, vmem_limit_bytes=54 * 2**20),

time: 26.6 us -> 25.4 us (0.955)
  Pallas kernels: 26.5 us -> 25.2 us
    pallas_call x1, Pallas kernels: 24 us -> 22.7 us  [shards(): pl.pallas_call(functools.partial(comm_kernel, (frames, rows // xdim, xdim...]
where the time goes in v2:
time: 25.4 us; the launch traced here: 25.2 us
  Pallas kernels  25.2 us (99%)
    pallas_call x1, Pallas kernels, shards(): pl.pallas_call(functools.partial(comm_kernel, (frames, rows // xdim, xdim...  22.7 us
    pallas_call x1, Pallas kernels, shards(): pl.pallas_call(functools.partial(conv_kernel, rows), out_shape=jax.ShapeD...  2.51 us

profile of v2, /device:TPU:1, one launch (start us, length us, event | category | flops | bytes accessed | tf_op | source)
XLA Modules:
  0.0 25.2 jit_solution(8960551577369178145)
XLA Ops:
  0.0 22.7 %statistics.1 = (bf16[3,192,256]{2,1,0:T(8,128)(2,1)S(1)}, f32[2,256]{1,0:T(2,128)S(1)}, bf16[4,3072,256]{2,1,0:T(8,128)(2,1)S(1)}) custom-call(bf16[2,96,256]{2,1,0:T(8,128)(2,1)} %bitcast.5, bf16[27,256,256]{2,1,0:T(8,128)(2,1)} %bitcast.4, f32[1,256]{1,0:T(1,128)} %bitcast.6), custom_call_target="tpu_custom_call" | custom-call | tf_op jit(solution)/shard_map/statistics/pallas_call | solution.py:375
  22.7 2.5 %conv.1 = bf16[4,4,2,48,256]{4,3,2,1,0:T(8,128)(2,1)} custom-call(bf16[3,192,256]{2,1,0:T(8,128)(2,1)S(1)} %get-tuple-element.8.halo, f32[2,256]{1,0:T(2,128)S(1)} %get-tuple-element.9.stat, bf16[4,3072,256]{2,1,0:T(8,128)(2,1)S(1)} %get-tuple-element.10.folded), custom_call_target="tpu_custom_call" | custom-call | tf_op jit(solution)/shard_map/conv/pallas_call | solution.py:401

commit v3 on v2

--- a/solution.py
+++ b/solution.py
@@ -10,7 +10,7 @@
 MESH = pl.DeviceIdType.MESH
 GROUP = 8
 F32, BF16 = jnp.float32, jnp.bfloat16
-ROOT = 1
+ROOT, AIDE = 1, 3
 LATE = 6
 
 
@@ -43,18 +43,9 @@
     return packed[0:1]
 
 
-def merged(parts, count):
-    total = jnp.sum(parts, axis=0)
-    mean = total * (1.0 / parts.shape[0])
-    apart = jnp.sum(jnp.square(parts - mean[None]), axis=0)
-    apart = pltpu.roll(jnp.broadcast_to(apart, (8, 128)), 2, 1)[0:1]
-    kind = lane_index((1, 128)) & 7
-    return jnp.where(kind < 2, mean, total + count * apart)
-
-
 def comm_kernel(
     shape, feat, weight, gain, halo_out, stat_out, folded,
-    raw, held, scale, msg1, buf1, lines, final,
+    raw, held, scale, msg1, buf1, final,
     in_sem, send1, recv1, send3, recv3, halo_send, halo_recv, ready,
 ):
     frames, ydim, xdim, total = shape
@@ -62,6 +53,9 @@
     f, r = lax.axis_index("frame"), lax.axis_index("row")
     y, x = r // xdim, r % xdim
     is_root = f == ROOT
+    is_aide = (f == AIDE) & (r == 0)
+    is_hub = is_root | is_aide
+    passes_on = (is_root & (r > 0)) | is_aide
 
     loads = [
         pltpu.make_async_copy(feat.at[t, part], held.at[1 + t, pl.ds(48 + part.start, 48)], in_sem.at[2 + 2 * t + i])
@@ -79,10 +73,10 @@
     def plane(i):
         return ((y + i // xdim) % ydim) * xdim + (x + i) % xdim
 
-    def to_root(i):
+    def share_to(frame, row):
         return pltpu.make_async_remote_copy(
             src_ref=msg1, dst_ref=buf1.at[f, r], send_sem=send1, recv_sem=recv1.at[f],
-            device_id=(ROOT, plane(i)), device_id_type=MESH,
+            device_id=(frame, row), device_id_type=MESH,
         )
 
     barrier = pltpu.get_barrier_semaphore()
@@ -111,6 +105,14 @@
         @pl.when(above_later)
         def _():
             greet(f, above)
+
+    @pl.when(is_aide)
+    def _():
+        def greet_root(k, carry):
+            greet(ROOT, k)
+            return carry
+
+        lax.fori_loop(0, rows, greet_root, 0)
 
     for load in loads:
         load.wait()
@@ -118,24 +120,32 @@
     mine = local_statistics(values, 192)
     msg1[...] = mine
     pl.semaphore_wait(barrier, jnp.where(
-        is_root, rows - 1, 3 - below_later.astype(jnp.int32) - above_later.astype(jnp.int32)))
+        is_root, rows, 3 - below_later.astype(jnp.int32) - above_later.astype(jnp.int32)))
 
     @pl.when(is_root)
     def _():
-        buf1[ROOT, r] = mine
         greet(0, r)
         lax.fori_loop(ROOT + 1, frames, greet_line, 0)
 
+    @pl.when(is_hub)
+    def _():
+        buf1[f, r] = mine
+
     @pl.when(jnp.logical_not(is_root))
     def _():
-        to_root(0).start()
-
-    def to_others(i, carry):
-        to_root(i).start()
+        share_to(ROOT, r).start()
+
+    def to_roots(i, carry):
+        share_to(ROOT, plane(i)).start()
         return carry
 
-    lax.fori_loop(rows // 2, rows, to_others, 0)
-    lax.fori_loop(1, rows // 2, to_others, 0)
+    lax.fori_loop(rows // 2, rows, to_roots, 0)
+
+    @pl.when(jnp.logical_not(is_aide))
+    def _():
+        share_to(AIDE, 0).start()
+
+    lax.fori_loop(1, rows // 2, to_roots, 0)
 
     fetch = pltpu.make_async_copy(weight, raw, in_sem.at[0])
     fetch.start()
@@ -211,9 +221,6 @@
         device_id=((f + 1) % frames, r), device_id_type=MESH,
     )
 
-    def arrived(k):
-        pltpu.make_async_copy(buf1.at[k], buf1.at[k], recv1.at[k]).wait()
-
     def pass_on():
         @pl.when(f + 1 < frames)
         def _():
@@ -230,51 +237,70 @@
         halo_out[...] = held[...]
 
     others = buf1.at[ROOT, 0:rows - 1]
-    heard = final.at[0:frames - 1]
-
-    @pl.when(is_root)
-    def _():
-        def gather(k):
-            lines[k] = merged(buf1[k], 192.0 * GROUP)
-
-        def tell(k):
-            pl.semaphore_signal(ready, inc=1, device_id=(k - 1, r), device_id_type=MESH)
-
-        pltpu.make_async_copy(others, others, recv1.at[ROOT]).wait()
-        gather(ROOT)
-        for k in (0, ROOT + 1):
+
+    @pl.when(is_hub)
+    def _():
+        is_mean = (lane_index((1, 128)) & 7) < 2
+        pivot = jnp.where(is_mean, mine, 0.0)
+
+        def arrived(k):
+            @pl.when(k != f)
+            def _():
+                pltpu.make_async_copy(buf1.at[k], buf1.at[k], recv1.at[k]).wait()
+
+            @pl.when(k == f)
+            def _():
+                pltpu.make_async_copy(others, others, recv1.at[k]).wait()
+
+            @pl.when(is_root & (k > ROOT + 1))
+            def _():
+                pl.semaphore_signal(ready, inc=1, device_id=(k - 1, r), device_id_type=MESH)
+
+        def gather(k, sums):
+            shares = buf1[k] - pivot[None]
+            return sums[0] + jnp.sum(shares, axis=0), sums[1] + jnp.sum(jnp.square(shares), axis=0)
+
+        def collect(k, sums):
             arrived(k)
-            gather(k)
-        pass_on()
-
-        def collect(k, carry):
+            return gather(k, sums)
+
+        sums = (jnp.zeros((1, 128), F32), jnp.zeros((1, 128), F32))
+        sums = lax.fori_loop(0, ROOT + 2, collect, sums)
+
+        @pl.when(is_root)
+        def _():
+            pass_on()
+
+        sums = lax.fori_loop(ROOT + 2, frames - LATE, collect, sums)
+
+        @pl.when(is_aide)
+        def _():
+            pl.semaphore_wait(ready, 1)
+            pass_on()
+
+        for k in range(frames - LATE, frames):
             arrived(k)
-            tell(k)
-            gather(k)
+        for k in range(frames - LATE, frames):
+            sums = gather(k, sums)
+        share = sums[0] * (1.0 / (frames * rows))
+        apart = jnp.broadcast_to(sums[1] - sums[0] * share, (8, 128))
+        final[0] = jnp.where(is_mean, pivot + share, sums[0] + 192.0 * GROUP * pltpu.roll(apart, 2, 1)[0:1])
+
+    @pl.when(passes_on)
+    def _():
+        def send_third(k, carry):
+            @pl.when((k != ROOT) & (k != f))
+            def _():
+                pltpu.make_async_remote_copy(
+                    src_ref=final.at[0], dst_ref=final.at[0], send_sem=send3, recv_sem=recv3,
+                    device_id=(k, r), device_id_type=MESH,
+                ).start()
+
             return carry
 
-        def collect_late(k, carry):
-            arrived(k)
-            tell(k)
-            return carry
-
-        lax.fori_loop(ROOT + 2, frames - LATE, collect, 0)
-        lax.fori_loop(frames - LATE, frames, collect_late, 0)
-        for k in range(frames - LATE, frames):
-            gather(k)
-        final[0] = merged(lines[...], 192.0 * GROUP * rows)
-
-        def send_third(k, carry):
-            pltpu.make_async_remote_copy(
-                src_ref=final.at[0], dst_ref=final.at[0], send_sem=send3, recv_sem=recv3,
-                device_id=(k, r), device_id_type=MESH,
-            ).start()
-            return carry
-
-        send_third(0, 0)
-        lax.fori_loop(ROOT + 1, frames, send_third, 0)
-
-    @pl.when(jnp.logical_not(is_root))
+        lax.fori_loop(0, frames, send_third, 0)
+
+    @pl.when(jnp.logical_not(is_hub))
     def _():
         @pl.when((f > ROOT) & (f + 1 < frames))
         def _():
@@ -295,14 +321,22 @@
     stat_out[0:1] = jnp.concatenate(spread[:2], axis=1)
     stat_out[1:2] = lax.rsqrt(var + 1e-06) * scale[...]
 
-    @pl.when(jnp.logical_not(is_root))
-    def _():
-        pltpu.make_async_copy(buf1.at[0], buf1.at[0], send1).wait()
-
-    @pl.when(is_root)
-    def _():
-        pltpu.make_async_copy(others, others, send1).wait()
+    @pl.when(jnp.logical_not(is_hub))
+    def _():
+        everyone = buf1.at[0, 0:1]
+        pltpu.make_async_copy(everyone, everyone, send1).wait()
+
+    every_root = buf1.at[0]
+    pltpu.make_async_copy(every_root, every_root, send1).wait()
+
+    @pl.when(passes_on)
+    def _():
+        heard = final.at[0:frames - 2]
         pltpu.make_async_copy(heard, heard, send3).wait()
+
+    @pl.when(passes_on & is_root)
+    def _():
+        pltpu.make_async_copy(final.at[0], final.at[0], send3).wait()
 
     down.wait_send()
     up.wait_send()
@@ -383,7 +417,6 @@
                 pltpu.VMEM((1, 256), F32),
                 pltpu.VMEM((1, 128), F32),
                 pltpu.VMEM((frames, rows, 1, 128), F32),
-                pltpu.VMEM((frames, 1, 128), F32),
                 pltpu.VMEM((frames - 1, 1, 128), F32),
                 pltpu.SemaphoreType.DMA((6,)),
                 pltpu.SemaphoreType.DMA,

time: 25.4 us -> 24.5 us (0.965)
  Pallas kernels: 25.2 us -> 24.3 us
    pallas_call x1, Pallas kernels: 22.7 us -> 21.8 us  [shards(): pl.pallas_call(functools.partial(comm_kernel, (frames, rows // xdim, xdim...]
where the time goes in v3:
time: 24.5 us; the launch traced here: 24.3 us
  Pallas kernels  24.3 us (99%)
    pallas_call x1, Pallas kernels, shards(): pl.pallas_call(functools.partial(comm_kernel, (frames, rows // xdim, xdim...  21.8 us
    pallas_call x1, Pallas kernels, shards(): pl.pallas_call(functools.partial(conv_kernel, rows), out_shape=jax.ShapeD...  2.51 us

profile of v3, /device:TPU:1, one launch (start us, length us, event | category | flops | bytes accessed | tf_op | source)
XLA Modules:
  0.0 24.3 jit_solution(6353015746991727651)
XLA Ops:
  0.0 21.8 %statistics.1 = (bf16[3,192,256]{2,1,0:T(8,128)(2,1)S(1)}, f32[2,256]{1,0:T(2,128)S(1)}, bf16[4,3072,256]{2,1,0:T(8,128)(2,1)S(1)}) custom-call(bf16[2,96,256]{2,1,0:T(8,128)(2,1)} %bitcast.5, bf16[27,256,256]{2,1,0:T(8,128)(2,1)} %bitcast.4, f32[1,256]{1,0:T(1,128)} %bitcast.6), custom_call_target="tpu_custom_call" | custom-call | tf_op jit(solution)/shard_map/statistics/pallas_call | solution.py:409
  21.8 2.5 %conv.1 = bf16[4,4,2,48,256]{4,3,2,1,0:T(8,128)(2,1)} custom-call(bf16[3,192,256]{2,1,0:T(8,128)(2,1)S(1)} %get-tuple-element.8.halo, f32[2,256]{1,0:T(2,128)S(1)} %get-tuple-element.9.stat, bf16[4,3072,256]{2,1,0:T(8,128)(2,1)S(1)} %get-tuple-element.10.folded), custom_call_target="tpu_custom_call" | custom-call | tf_op jit(solution)/shard_map/conv/pallas_call | solution.py:434

commit v4 on v3

--- a/solution.py
+++ b/solution.py
@@ -25,10 +25,13 @@
 
 def local_statistics(own, rows):
     count = float(rows)
-    mean = jnp.sum(own, axis=0, keepdims=True) * (1.0 / count)
-    spread = jnp.sum(jnp.square(own - mean), axis=0, keepdims=True)
+    pivot = own[0:1]
+    apart = own - pivot
+    offset = jnp.sum(apart, axis=0, keepdims=True)
+    spread = jnp.sum(jnp.square(apart), axis=0, keepdims=True) - offset * offset * (1.0 / count)
+    mean = pivot + offset * (1.0 / count)
     packed = jnp.zeros((8, 128), F32)
-    kind = lane_index((8, 128)) & 7
+    kind = lane_index((8, 128)) & 3
     for half in range(2):
         lanes = slice(128 * half, 128 * half + 128)
         m = jnp.broadcast_to(mean[:, lanes], (8, 128))
@@ -75,7 +78,7 @@
 
     def share_to(frame, row):
         return pltpu.make_async_remote_copy(
-            src_ref=msg1, dst_ref=buf1.at[f, r], send_sem=send1, recv_sem=recv1.at[f],
+            src_ref=msg1, dst_ref=buf1.at[f, pl.ds(r, 1)], send_sem=send1, recv_sem=recv1.at[f],
             device_id=(frame, row), device_id_type=MESH,
         )
 
@@ -129,7 +132,7 @@
 
     @pl.when(is_hub)
     def _():
-        buf1[f, r] = mine
+        buf1[f, pl.ds(r, 1)] = mine
 
     @pl.when(jnp.logical_not(is_root))
     def _():
@@ -240,7 +243,7 @@
 
     @pl.when(is_hub)
     def _():
-        is_mean = (lane_index((1, 128)) & 7) < 2
+        is_mean = (lane_index((1, 128)) & 3) < 2
         pivot = jnp.where(is_mean, mine, 0.0)
 
         def arrived(k):
@@ -257,14 +260,14 @@
                 pl.semaphore_signal(ready, inc=1, device_id=(k - 1, r), device_id_type=MESH)
 
         def gather(k, sums):
-            shares = buf1[k] - pivot[None]
+            shares = (buf1[k] - pivot).reshape(rows // 8, 8, 128)
             return sums[0] + jnp.sum(shares, axis=0), sums[1] + jnp.sum(jnp.square(shares), axis=0)
 
         def collect(k, sums):
             arrived(k)
             return gather(k, sums)
 
-        sums = (jnp.zeros((1, 128), F32), jnp.zeros((1, 128), F32))
+        sums = (jnp.zeros((8, 128), F32), jnp.zeros((8, 128), F32))
         sums = lax.fori_loop(0, ROOT + 2, collect, sums)
 
         @pl.when(is_root)
@@ -282,9 +285,10 @@
             arrived(k)
         for k in range(frames - LATE, frames):
             sums = gather(k, sums)
-        share = sums[0] * (1.0 / (frames * rows))
-        apart = jnp.broadcast_to(sums[1] - sums[0] * share, (8, 128))
-        final[0] = jnp.where(is_mean, pivot + share, sums[0] + 192.0 * GROUP * pltpu.roll(apart, 2, 1)[0:1])
+        offset = jnp.sum(sums[0], axis=0, keepdims=True)
+        share = offset * (1.0 / (frames * rows))
+        apart = jnp.broadcast_to(jnp.sum(sums[1], axis=0, keepdims=True) - offset * share, (8, 128))
+        final[0] = jnp.where(is_mean, pivot + share, offset + 192.0 * GROUP * pltpu.roll(apart, 2, 1)[0:1])
 
     @pl.when(passes_on)
     def _():
@@ -310,12 +314,14 @@
         pltpu.make_async_copy(final.at[0], final.at[0], recv3).wait()
 
     line = jnp.broadcast_to(final[0], (8, 128))
-    kind = lane_index((8, 128)) & 7
+    kind = lane_index((8, 128)) & 3
+    by_one = swapped(line, 1)
+    near = (line, by_one, swapped(line, 2), swapped(by_one, 2))
     spread = []
     for k in range(4):
-        v = jnp.where(kind == k, line, 0.0)
-        for distance in (1, 2, 4):
-            v = v + swapped(v, distance)
+        v = near[0]
+        for distance in range(1, 4):
+            v = jnp.where((kind ^ k) == distance, near[distance], v)
         spread.append(v[0:1])
     var = jnp.concatenate(spread[2:], axis=1) * (1.0 / total)
     stat_out[0:1] = jnp.concatenate(spread[:2], axis=1)
@@ -416,7 +422,7 @@
                 pltpu.VMEM((3, 192, 256), BF16),
                 pltpu.VMEM((1, 256), F32),
                 pltpu.VMEM((1, 128), F32),
-                pltpu.VMEM((frames, rows, 1, 128), F32),
+                pltpu.VMEM((frames, rows, 128), F32),
                 pltpu.VMEM((frames - 1, 1, 128), F32),
                 pltpu.SemaphoreType.DMA((6,)),
                 pltpu.SemaphoreType.DMA,

time: 24.5 us -> 24.2 us (0.988)
  Pallas kernels: 24.3 us -> 24 us
    pallas_call x1, Pallas kernels: 21.8 us -> 21.5 us  [shards(): pl.pallas_call(functools.partial(comm_kernel, (frames, rows // xdim, xdim...]
where the time goes in v4:
time: 24.2 us; the launch traced here: 24 us
  Pallas kernels  24 us (99%)
    pallas_call x1, Pallas kernels, shards(): pl.pallas_call(functools.partial(comm_kernel, (frames, rows // xdim, xdim...  21.5 us
    pallas_call x1, Pallas kernels, shards(): pl.pallas_call(functools.partial(conv_kernel, rows), out_shape=jax.ShapeD...  2.51 us

profile of v4, /device:TPU:1, one launch (start us, length us, event | category | flops | bytes accessed | tf_op | source)
XLA Modules:
  0.0 24.0 jit_solution(1550849553961976381)
XLA Ops:
  0.0 21.5 %statistics.1 = (bf16[3,192,256]{2,1,0:T(8,128)(2,1)S(1)}, f32[2,256]{1,0:T(2,128)S(1)}, bf16[4,3072,256]{2,1,0:T(8,128)(2,1)S(1)}) custom-call(bf16[2,96,256]{2,1,0:T(8,128)(2,1)} %bitcast.5, bf16[27,256,256]{2,1,0:T(8,128)(2,1)} %bitcast.4, f32[1,256]{1,0:T(1,128)} %bitcast.6), custom_call_target="tpu_custom_call" | custom-call | tf_op jit(solution)/shard_map/statistics/pallas_call | solution.py:415
  21.5 2.5 %conv.1 = bf16[4,4,2,48,256]{4,3,2,1,0:T(8,128)(2,1)} custom-call(bf16[3,192,256]{2,1,0:T(8,128)(2,1)S(1)} %get-tuple-element.8.halo, f32[2,256]{1,0:T(2,128)S(1)} %get-tuple-element.9.stat, bf16[4,3072,256]{2,1,0:T(8,128)(2,1)S(1)} %get-tuple-element.10.folded), custom_call_target="tpu_custom_call" | custom-call | tf_op jit(solution)/shard_map/conv/pallas_call | solution.py:440

commit v5 on v4

--- a/solution.py
+++ b/solution.py
@@ -259,22 +259,17 @@
             def _():
                 pl.semaphore_signal(ready, inc=1, device_id=(k - 1, r), device_id_type=MESH)
 
-        def gather(k, sums):
-            shares = (buf1[k] - pivot).reshape(rows // 8, 8, 128)
-            return sums[0] + jnp.sum(shares, axis=0), sums[1] + jnp.sum(jnp.square(shares), axis=0)
-
-        def collect(k, sums):
+        def collect(k, carry):
             arrived(k)
-            return gather(k, sums)
-
-        sums = (jnp.zeros((8, 128), F32), jnp.zeros((8, 128), F32))
-        sums = lax.fori_loop(0, ROOT + 2, collect, sums)
+            return carry
+
+        lax.fori_loop(0, ROOT + 2, collect, 0)
 
         @pl.when(is_root)
         def _():
             pass_on()
 
-        sums = lax.fori_loop(ROOT + 2, frames - LATE, collect, sums)
+        lax.fori_loop(ROOT + 2, frames - LATE, collect, 0)
 
         @pl.when(is_aide)
         def _():
@@ -283,8 +278,8 @@
 
         for k in range(frames - LATE, frames):
             arrived(k)
-        for k in range(frames - LATE, frames):
-            sums = gather(k, sums)
+        shares = (buf1[...] - pivot).reshape(frames * rows // 8, 8, 128)
+        sums = jnp.sum(shares, axis=0), jnp.sum(jnp.square(shares), axis=0)
         offset = jnp.sum(sums[0], axis=0, keepdims=True)
         share = offset * (1.0 / (frames * rows))
         apart = jnp.broadcast_to(jnp.sum(sums[1], axis=0, keepdims=True) - offset * share, (8, 128))
@@ -382,13 +377,18 @@
     copies = []
     for p in range(2):
         for q in range(2):
-            def taps(kind):
-                return [piece(kind, p + a, q + b) for a in range(2) for b in range(2)]
-
-            first = jnp.dot(jnp.concatenate(taps(0) + taps(1), axis=1), folded[p * 2 + q, 0:2048],
-                            preferred_element_type=F32)
-            step = jnp.dot(jnp.concatenate(taps(2), axis=1), folded[p * 2 + q, 2048:3072],
-                           preferred_element_type=F32)
+            def product(kinds):
+                total = None
+                for kind in kinds:
+                    for a in range(2):
+                        for b in range(2):
+                            at = kind * 1024 + (a * 2 + b) * 256
+                            term = jnp.dot(piece(kind, p + a, q + b), folded[p * 2 + q, at:at + 256],
+                                           preferred_element_type=F32)
+                            total = term if total is None else total + term
+                return total
+
+            first, step = product((0, 1)), product((2,))
             second = first + step
             for i in range(2):
                 for alpha, v in enumerate((first, second)):
@@ -396,11 +396,15 @@
                         lanes = slice(128 * half, 128 * half + 128)
                         wide[half, 2 * i + alpha, :, pl.ds(q, 24, 2), :] = v[96 * i:96 * i + 96, lanes].reshape(
                             4, 24, 128)
-        for half in range(2):
-            staged[p, :, :, :, 128 * half:128 * half + 128] = wide[half].astype(BF16)
-        copy = pltpu.make_async_copy(staged.at[p], out.at[:, :, p], out_sem.at[p])
-        copy.start()
-        copies.append(copy)
+        size = 4 if p == 0 else 1
+        for at in range(0, 4, size):
+            part = slice(at, at + size)
+            for half in range(2):
+                lanes = slice(128 * half, 128 * half + 128)
+                staged[p, part, :, :, lanes] = wide[half, part, :, 0:48].astype(BF16)
+            copy = pltpu.make_async_copy(staged.at[p, part], out.at[part, :, p], out_sem.at[p, at])
+            copy.start()
+            copies.append(copy)
     for copy in copies:
         copy.wait()
 
@@ -446,9 +450,9 @@
                 pltpu.VMEM((3, 6, 40, 256), F32),
                 pltpu.VMEM((3, 5, 144, 256), BF16),
                 pltpu.VMEM((3, 5, 96, 256), BF16),
-                pltpu.VMEM((2, 4, 4, 48, 128), F32),
+                pltpu.VMEM((2, 4, 4, 56, 128), F32),
                 pltpu.VMEM((2, 4, 4, 48, 256), BF16),
-                pltpu.SemaphoreType.DMA((2,)),
+                pltpu.SemaphoreType.DMA((2, 4)),
             ],
             compiler_params=pltpu.CompilerParams(vmem_limit_bytes=24 * 2**20),
             name="conv",

time: 24.2 us -> 24.1 us (level)
  no operation moved by 1% of the time
where the time goes in v5:
time: 24.1 us; the launch traced here: 23.9 us
  Pallas kernels  23.9 us (99%)
    pallas_call x1, Pallas kernels, shards(): pl.pallas_call(functools.partial(comm_kernel, (frames, rows // xdim, xdim...  21.5 us
    pallas_call x1, Pallas kernels, shards(): pl.pallas_call(functools.partial(conv_kernel, rows), out_shape=jax.ShapeD...  2.43 us

profile of v5, /device:TPU:1, one launch (start us, length us, event | category | flops | bytes accessed | tf_op | source)
XLA Modules:
  0.0 23.9 jit_solution(4149442249700454220)
XLA Ops:
  0.0 21.5 %statistics.1 = (bf16[3,192,256]{2,1,0:T(8,128)(2,1)S(1)}, f32[2,256]{1,0:T(2,128)S(1)}, bf16[4,3072,256]{2,1,0:T(8,128)(2,1)S(1)}) custom-call(bf16[2,96,256]{2,1,0:T(8,128)(2,1)} %bitcast.5, bf16[27,256,256]{2,1,0:T(8,128)(2,1)} %bitcast.4, f32[1,256]{1,0:T(1,128)} %bitcast.6), custom_call_target="tpu_custom_call" | custom-call | tf_op jit(solution)/shard_map/statistics/pallas_call | solution.py:419
  21.5 2.4 %conv.1 = bf16[4,4,2,48,256]{4,3,2,1,0:T(8,128)(2,1)} custom-call(bf16[3,192,256]{2,1,0:T(8,128)(2,1)S(1)} %get-tuple-element.8.halo, f32[2,256]{1,0:T(2,128)S(1)} %get-tuple-element.9.stat, bf16[4,3072,256]{2,1,0:T(8,128)(2,1)S(1)} %get-tuple-element.10.folded), custom_call_target="tpu_custom_call" | custom-call | tf_op jit(solution)/shard_map/conv/pallas_call | solution.py:444

commit v6 on v5

--- a/solution.py
+++ b/solution.py
@@ -21,6 +21,16 @@
 def swapped(value, distance):
     upper = (lane_index(value.shape) & distance) == 0
     return jnp.where(upper, pltpu.roll(value, 128 - distance, 1), pltpu.roll(value, distance, 1))
+
+
+def quad(value):
+    lane = lane_index(value.shape) & 3
+    after = [pltpu.roll(value, 128 - d, 1) for d in (1, 2, 3)]
+    before = [pltpu.roll(value, d, 1) for d in (1, 2, 3)]
+    one = jnp.where((lane & 1) == 0, after[0], before[0])
+    two = jnp.where(lane < 2, after[1], before[1])
+    three = jnp.where(lane == 0, after[2], jnp.where(lane == 3, before[2], jnp.where(lane == 1, after[0], before[0])))
+    return value, one, two, three
 
 
 def local_statistics(own, rows):
@@ -30,20 +40,20 @@
     offset = jnp.sum(apart, axis=0, keepdims=True)
     spread = jnp.sum(jnp.square(apart), axis=0, keepdims=True) - offset * offset * (1.0 / count)
     mean = pivot + offset * (1.0 / count)
-    packed = jnp.zeros((8, 128), F32)
-    kind = lane_index((8, 128)) & 3
-    for half in range(2):
-        lanes = slice(128 * half, 128 * half + 128)
-        m = jnp.broadcast_to(mean[:, lanes], (8, 128))
-        s = jnp.broadcast_to(spread[:, lanes], (8, 128))
-        held = count
-        for distance in (1, 2, 4):
-            other_m, other_s = swapped(m, distance), swapped(s, distance)
-            s = s + other_s + (0.5 * held) * jnp.square(m - other_m)
-            m = 0.5 * (m + other_m)
-            held *= 2.0
-        packed = jnp.where(kind == half, m, jnp.where(kind == 2 + half, s, packed))
-    return packed[0:1]
+    low = lax.broadcasted_iota(jnp.int32, (8, 128), 0) == 0
+
+    def halves(v):
+        return jnp.where(low, jnp.broadcast_to(v[:, 0:128], (8, 128)), jnp.broadcast_to(v[:, 128:256], (8, 128)))
+
+    means, spreads = quad(halves(mean)), quad(halves(spread))
+    m = 0.25 * ((means[0] + means[1]) + (means[2] + means[3]))
+    s = (spreads[0] + spreads[1]) + (spreads[2] + spreads[3])
+    s = s + count * sum(jnp.square(v - m) for v in means)
+    other_m, other_s = swapped(m, 4), swapped(s, 4)
+    s = s + other_s + (2.0 * count) * jnp.square(m - other_m)
+    m = 0.5 * (m + other_m)
+    kind = lane_index((1, 128)) & 3
+    return jnp.where(kind == 0, m[0:1], jnp.where(kind == 1, m[1:2], jnp.where(kind == 2, s[0:1], s[1:2])))
 
 
 def comm_kernel(
@@ -282,8 +292,8 @@
         sums = jnp.sum(shares, axis=0), jnp.sum(jnp.square(shares), axis=0)
         offset = jnp.sum(sums[0], axis=0, keepdims=True)
         share = offset * (1.0 / (frames * rows))
-        apart = jnp.broadcast_to(jnp.sum(sums[1], axis=0, keepdims=True) - offset * share, (8, 128))
-        final[0] = jnp.where(is_mean, pivot + share, offset + 192.0 * GROUP * pltpu.roll(apart, 2, 1)[0:1])
+        final[0, 0:1] = jnp.where(is_mean, pivot + share, offset)
+        final[0, 1:2] = jnp.sum(sums[1], axis=0, keepdims=True) - offset * share
 
     @pl.when(passes_on)
     def _():
@@ -308,16 +318,17 @@
         pass_on()
         pltpu.make_async_copy(final.at[0], final.at[0], recv3).wait()
 
-    line = jnp.broadcast_to(final[0], (8, 128))
     kind = lane_index((8, 128)) & 3
-    by_one = swapped(line, 1)
-    near = (line, by_one, swapped(line, 2), swapped(by_one, 2))
-    spread = []
-    for k in range(4):
+    line, apart = (quad(jnp.broadcast_to(final[0, i:i + 1], (8, 128))) for i in range(2))
+
+    def everywhere(near, k):
         v = near[0]
         for distance in range(1, 4):
             v = jnp.where((kind ^ k) == distance, near[distance], v)
-        spread.append(v[0:1])
+        return v[0:1]
+
+    spread = [everywhere(line, 0), everywhere(line, 1)]
+    spread += [everywhere(line, 2 + h) + 192.0 * GROUP * everywhere(apart, h) for h in range(2)]
     var = jnp.concatenate(spread[2:], axis=1) * (1.0 / total)
     stat_out[0:1] = jnp.concatenate(spread[:2], axis=1)
     stat_out[1:2] = lax.rsqrt(var + 1e-06) * scale[...]
@@ -427,7 +438,7 @@
                 pltpu.VMEM((1, 256), F32),
                 pltpu.VMEM((1, 128), F32),
                 pltpu.VMEM((frames, rows, 128), F32),
-                pltpu.VMEM((frames - 1, 1, 128), F32),
+                pltpu.VMEM((frames - 1, 2, 128), F32),
                 pltpu.SemaphoreType.DMA((6,)),
                 pltpu.SemaphoreType.DMA,
                 pltpu.SemaphoreType.DMA((frames,)),

time: 24.1 us -> 23.9 us (level)
  no operation moved by 1% of the time
where the time goes in v6:
time: 23.9 us; the launch traced here: 23.7 us
  Pallas kernels  23.7 us (99%)
    pallas_call x1, Pallas kernels, shards(): pl.pallas_call(functools.partial(comm_kernel, (frames, rows // xdim, xdim...  21.3 us
    pallas_call x1, Pallas kernels, shards(): pl.pallas_call(functools.partial(conv_kernel, rows), out_shape=jax.ShapeD...  2.43 us

profile of v6, /device:TPU:1, one launch (start us, length us, event | category | flops | bytes accessed | tf_op | source)
XLA Modules:
  0.0 23.7 jit_solution(14879426546136162322)
XLA Ops:
  0.0 21.3 %statistics.1 = (bf16[3,192,256]{2,1,0:T(8,128)(2,1)S(1)}, f32[2,256]{1,0:T(2,128)S(1)}, bf16[4,3072,256]{2,1,0:T(8,128)(2,1)S(1)}) custom-call(bf16[2,96,256]{2,1,0:T(8,128)(2,1)} %bitcast.5, bf16[27,256,256]{2,1,0:T(8,128)(2,1)} %bitcast.4, f32[1,256]{1,0:T(1,128)} %bitcast.6), custom_call_target="tpu_custom_call" | custom-call | tf_op jit(solution)/shard_map/statistics/pallas_call | solution.py:430
  21.3 2.4 %conv.1 = bf16[4,4,2,48,256]{4,3,2,1,0:T(8,128)(2,1)} custom-call(bf16[3,192,256]{2,1,0:T(8,128)(2,1)S(1)} %get-tuple-element.8.halo, f32[2,256]{1,0:T(2,128)S(1)} %get-tuple-element.9.stat, bf16[4,3072,256]{2,1,0:T(8,128)(2,1)S(1)} %get-tuple-element.10.folded), custom_call_target="tpu_custom_call" | custom-call | tf_op jit(solution)/shard_map/conv/pallas_call | solution.py:455

commit v7 on v6

--- a/solution.py
+++ b/solution.py
@@ -11,7 +11,7 @@
 GROUP = 8
 F32, BF16 = jnp.float32, jnp.bfloat16
 ROOT, AIDE = 1, 3
-LATE = 6
+LATE = 8
 
 
 def lane_index(shape):
@@ -287,7 +287,12 @@
             pass_on()
 
         for k in range(frames - LATE, frames):
-            arrived(k)
+            pltpu.make_async_copy(buf1.at[k], buf1.at[k], recv1.at[k]).wait()
+
+            @pl.when(is_root)
+            def _():
+                pl.semaphore_signal(ready, inc=1, device_id=(k - 1, r), device_id_type=MESH)
+
         shares = (buf1[...] - pivot).reshape(frames * rows // 8, 8, 128)
         sums = jnp.sum(shares, axis=0), jnp.sum(jnp.square(shares), axis=0)
         offset = jnp.sum(sums[0], axis=0, keepdims=True)
@@ -403,19 +408,17 @@
             second = first + step
             for i in range(2):
                 for alpha, v in enumerate((first, second)):
+                    t = 2 * i + alpha
                     for half in range(2):
                         lanes = slice(128 * half, 128 * half + 128)
-                        wide[half, 2 * i + alpha, :, pl.ds(q, 24, 2), :] = v[96 * i:96 * i + 96, lanes].reshape(
-                            4, 24, 128)
-        size = 4 if p == 0 else 1
-        for at in range(0, 4, size):
-            part = slice(at, at + size)
-            for half in range(2):
-                lanes = slice(128 * half, 128 * half + 128)
-                staged[p, part, :, :, lanes] = wide[half, part, :, 0:48].astype(BF16)
-            copy = pltpu.make_async_copy(staged.at[p, part], out.at[part, :, p], out_sem.at[p, at])
-            copy.start()
-            copies.append(copy)
+                        wide[half, t, :, pl.ds(q, 24, 2), :] = v[96 * i:96 * i + 96, lanes].reshape(4, 24, 128)
+                        if q == 1:
+                            staged[p, t, :, :, lanes] = wide[half, t, :, 0:48].astype(BF16)
+                    if q == 1 and (p == 1 or t == 3):
+                        part = slice(t, t + 1) if p == 1 else slice(0, 4)
+                        copy = pltpu.make_async_copy(staged.at[p, part], out.at[part, :, p], out_sem.at[p, t])
+                        copy.start()
+                        copies.append(copy)
     for copy in copies:
         copy.wait()
 

time: 23.9 us -> 23.9 us (level)
  no operation moved by 1% of the time
where the time goes in v7:
time: 23.9 us; the launch traced here: 23.7 us
  Pallas kernels  23.7 us (99%)
    pallas_call x1, Pallas kernels, shards(): pl.pallas_call(functools.partial(comm_kernel, (frames, rows // xdim, xdim...  21.3 us
    pallas_call x1, Pallas kernels, shards(): pl.pallas_call(functools.partial(conv_kernel, rows), out_shape=jax.ShapeD...  2.43 us

profile of v7, /device:TPU:1, one launch (start us, length us, event | category | flops | bytes accessed | tf_op | source)
XLA Modules:
  0.0 23.7 jit_solution(4562969687598831724)
XLA Ops:
  0.0 21.3 %statistics.1 = (bf16[3,192,256]{2,1,0:T(8,128)(2,1)S(1)}, f32[2,256]{1,0:T(2,128)S(1)}, bf16[4,3072,256]{2,1,0:T(8,128)(2,1)S(1)}) custom-call(bf16[2,96,256]{2,1,0:T(8,128)(2,1)} %bitcast.5, bf16[27,256,256]{2,1,0:T(8,128)(2,1)} %bitcast.4, f32[1,256]{1,0:T(1,128)} %bitcast.6), custom_call_target="tpu_custom_call" | custom-call | tf_op jit(solution)/shard_map/statistics/pallas_call | solution.py:433
  21.3 2.4 %conv.1 = bf16[4,4,2,48,256]{4,3,2,1,0:T(8,128)(2,1)} custom-call(bf16[3,192,256]{2,1,0:T(8,128)(2,1)S(1)} %get-tuple-element.8.halo, f32[2,256]{1,0:T(2,128)S(1)} %get-tuple-element.9.stat, bf16[4,3072,256]{2,1,0:T(8,128)(2,1)S(1)} %get-tuple-element.10.folded), custom_call_target="tpu_custom_call" | custom-call | tf_op jit(solution)/shard_map/conv/pallas_call | solution.py:458

commit v8 on v7

--- a/solution.py
+++ b/solution.py
@@ -45,13 +45,15 @@
     def halves(v):
         return jnp.where(low, jnp.broadcast_to(v[:, 0:128], (8, 128)), jnp.broadcast_to(v[:, 128:256], (8, 128)))
 
-    means, spreads = quad(halves(mean)), quad(halves(spread))
-    m = 0.25 * ((means[0] + means[1]) + (means[2] + means[3]))
-    s = (spreads[0] + spreads[1]) + (spreads[2] + spreads[3])
-    s = s + count * sum(jnp.square(v - m) for v in means)
-    other_m, other_s = swapped(m, 4), swapped(s, 4)
-    s = s + other_s + (2.0 * count) * jnp.square(m - other_m)
-    m = 0.5 * (m + other_m)
+    m, s = halves(mean), halves(spread)
+    lane = lane_index((8, 128)) & (GROUP - 1)
+    shifts = [(d, lane >= d) for d in range(1, GROUP)] + [(128 - d, lane + d < GROUP) for d in range(1, GROUP)]
+    rolled = [pltpu.roll(m, d, 1) for d, _ in shifts]
+    s = s + sum(jnp.where(inside, pltpu.roll(s, d, 1), 0.0) for d, inside in shifts)
+    center = (m + sum(jnp.where(inside, v, 0.0) for (_, inside), v in zip(shifts, rolled))) * (1.0 / GROUP)
+    apart = sum(jnp.where(inside, jnp.square(v - center), 0.0) for (_, inside), v in zip(shifts, rolled))
+    s = s + count * (jnp.square(m - center) + apart)
+    m = center
     kind = lane_index((1, 128)) & 3
     return jnp.where(kind == 0, m[0:1], jnp.where(kind == 1, m[1:2], jnp.where(kind == 2, s[0:1], s[1:2])))
 

time: 23.9 us -> 23.9 us (level)
  no operation moved by 1% of the time
where the time goes in v8:
time: 23.9 us; the launch traced here: 23.7 us
  Pallas kernels  23.7 us (99%)
    pallas_call x1, Pallas kernels, shards(): pl.pallas_call(functools.partial(comm_kernel, (frames, rows // xdim, xdim...  21.3 us
    pallas_call x1, Pallas kernels, shards(): pl.pallas_call(functools.partial(conv_kernel, rows), out_shape=jax.ShapeD...  2.43 us

profile of v8, /device:TPU:1, one launch (start us, length us, event | category | flops | bytes accessed | tf_op | source)
XLA Modules:
  0.0 23.7 jit_solution(6938347652634321113)
XLA Ops:
  0.0 21.3 %statistics.1 = (bf16[3,192,256]{2,1,0:T(8,128)(2,1)S(1)}, f32[2,256]{1,0:T(2,128)S(1)}, bf16[4,3072,256]{2,1,0:T(8,128)(2,1)S(1)}) custom-call(bf16[2,96,256]{2,1,0:T(8,128)(2,1)} %bitcast.5, bf16[27,256,256]{2,1,0:T(8,128)(2,1)} %bitcast.4, f32[1,256]{1,0:T(1,128)} %bitcast.6), custom_call_target="tpu_custom_call" | custom-call | tf_op jit(solution)/shard_map/statistics/pallas_call | solution.py:435
  21.3 2.4 %conv.1 = bf16[4,4,2,48,256]{4,3,2,1,0:T(8,128)(2,1)} custom-call(bf16[3,192,256]{2,1,0:T(8,128)(2,1)S(1)} %get-tuple-element.8.halo, f32[2,256]{1,0:T(2,128)S(1)} %get-tuple-element.9.stat, bf16[4,3072,256]{2,1,0:T(8,128)(2,1)S(1)} %get-tuple-element.10.folded), custom_call_target="tpu_custom_call" | custom-call | tf_op jit(solution)/shard_map/conv/pallas_call | solution.py:460
